TPU v7x, 32 devices: a whole 2x2x4 slice. The times are simulated.
32 devices in a mesh: occ: 2 (over x), vw: 8 (over z, y), vn: 2 (over core).
Axes of the slice: x: 2, y: 2, z: 4, core: 2. Of those that a mesh axis runs over, the one named last changes fastest.
Arguments:
- slabs: bfloat16 [2, 5120, 10240], P('occ', 'vw', 'vn'), may hold values from -0.125 to 0.125
- pair_list: int32 [1, 2], replicated, may hold values from 0 to 1
- occ_energy: float32 [2], replicated, may hold values from -1.2 to -0.4
- virt_energy: float32 [5120], replicated, may hold values from 0.2 to 2.5
Outputs:
- density: float32 [5120, 5120], P('vw', ('occ', 'vn'))
Inputs may be any that keep to these rules, and one draw needn't show every extreme that they name: `pair_list`: entries are orbital indices of the window; both entries of a pair may be equal.
All inputs are finite; a program needn't handle non-finite values.
Results may differ from a plain program's by a relative error of at most 0.0035.
Values may be sent and summed in bfloat16 or wider, within the bound.
No kernel may reach another device: no remote copies, remote signals or barrier semaphores. Data moves between devices by JAX's collectives and lax.ppermute only.
A program may use at most 128 MiB of HBM per device.

v0:
```python
import jax
import jax.numpy as jnp
from jax import lax
from jax.sharding import PartitionSpec as P


def contract_rows(left, piece):
    return lax.dot_general(
        left, piece, (((1,), (1,)), ((), ())), preferred_element_type=jnp.float32
    )


def per_device(slabs, pair_list, occ_energy, virt_energy):
    n_vw = lax.axis_size("vw")
    n_occ = lax.axis_size("occ")
    n_vn = lax.axis_size("vn")
    tile_rows = slabs.shape[1]
    sub_rows = tile_rows // n_occ
    my_occ = lax.axis_index("occ")
    my_vw = lax.axis_index("vw")
    my_vn = lax.axis_index("vn")
    row_energy = lax.dynamic_slice_in_dim(virt_energy, my_vw * tile_rows, tile_rows)
    energy_grid = virt_energy.reshape(n_vw, n_occ, sub_rows)
    col_energy = lax.dynamic_index_in_dim(energy_grid, my_occ, 1, keepdims=False).reshape(
        n_vw * sub_rows
    )
    share = n_vw * sub_rows // n_vn
    col_share = lax.dynamic_slice_in_dim(col_energy, my_vn * share, share)
    pieces = lax.all_to_all(slabs, "occ", split_axis=1, concat_axis=0, tiled=True)
    first = pair_list[0, 0]
    second = pair_list[0, 1]
    first_piece = lax.dynamic_index_in_dim(pieces, first, 0, keepdims=False)
    row_tile = lax.all_gather(first_piece, "occ", axis=0, tiled=True)
    col_piece = lax.dynamic_index_in_dim(pieces, second, 0, keepdims=False)
    integrals = contract_rows(row_tile, lax.all_gather(col_piece, "vw", axis=0, tiled=True))
    summed = lax.psum(integrals, "vn")
    mine = lax.dynamic_slice_in_dim(summed, my_vn * share, share, 1)
    denom = occ_energy[first] + occ_energy[second] - row_energy[:, None] - col_share[None, :]
    amplitude = (mine / denom).astype(jnp.bfloat16)
    density_part = contract_rows(amplitude, lax.all_gather(amplitude, "vw", axis=0, tiled=True))
    return lax.psum_scatter(density_part, ("occ", "vn"), scatter_dimension=1, tiled=True)


def solution(mesh):
    in_specs = (P("occ", "vw", "vn"), P(), P(), P())
    out_specs = P("vw", ("occ", "vn"))
    return jax.shard_map(
        per_device, mesh=mesh, in_specs=in_specs, out_specs=out_specs, check_vma=False
    )
```

profile of v0, /device:TPU:0, one launch (start us, length us, event | category | flops | bytes accessed | tf_op | source)
XLA Modules:
  0.0 1128.8 jit_solution(12539356711798565438)
XLA Ops:
  6.5 12.6 %copy.10 = bf16[1,640,5120]{2,0,1:T(2,128)(2,1)} copy(bf16[1,640,5120]{2,1,0:T(8,128)(2,1)} %param.4) | data formatting | bytes 13107200 | tf_op args[0]
  19.2 0.5 broadcast.4
  19.7 39.2 %reduce.2 = bf16[640,5120]{1,0:T(8,128)(2,1)} reduce(bf16[640,1,5120]{2,1,0:T(2,128)(2,1)} %bitcast.17, bf16[]{:T(256)} %broadcast.4), dimensions={1}, to_apply=%bitcast.16.reduce_sub_computation | reduce | bytes 13107202
  58.9 8.4 reshape.21
  67.3 0.0 copy-start.2
  67.3 6.5 all-to-all-start
  73.8 0.2 all-gather.8.cloned.1.call-start
  74.1 0.0 copy-done.2
  74.1 0.6 fusion.4
  76.6 71.4 %all-to-all-done = bf16[2,2,819200]{2,1,0:T(2,128)(2,1)} async-done(((bf16[2,2,819200]{2,1,0:T(2,128)(2,1)}), bf16[2,2,819200]{2,1,0:T(2,128)(2,1)}, u32[]{:S(2)}, u32[]{:S(2)}) %all-to-all-start) | async-done | bytes 6553632 | tf_op jit(solution)/shard_map/all_to_all | solution.py:29
  148.0 14.8 %reshape.22 = bf16[640,1,5120]{2,1,0:T(2,128)(2,1)} reshape(bf16[2,2,819200]{2,1,0:T(2,128)(2,1)} %all-to-all-done) | data formatting | bytes 13107200
  162.8 9.8 copy.7
  172.6 3.8 constant_dynamic-slice_fusion.1
  176.4 0.0 all-gather.8.cloned.1.call-update
  176.4 0.0 all-gather.10.cloned.1.call-start
  178.1 3.8 constant_dynamic-slice_fusion
  182.0 0.0 all-gather.10.cloned.1.call-update
  182.0 0.0 all-reduce.2.cloned.1.call-start
  182.0 78.4 %all-gather.8.cloned.1.call-done = bf16[1,1,640,5120]{3,2,1,0:T(8,128)(2,1)} async-done(((bf16[1,1,320,5120]{3,2,1,0:T(8,128)(2,1)}), bf16[1,1,640,5120]{3,2,1,0:T(8,128)(2,1)}) %all-gather.8.cloned.1.call-update) | async-done | bytes 6553616 | tf_op jit(solution)/shard_map/all_gather | solution.py:33
  260.4 501.7 %all-gather.10.cloned.1.call-done = bf16[1,2560,5120]{2,1,0:T(8,128)(2,1)} async-done(((bf16[1,320,5120]{2,1,0:T(8,128)(2,1)}), bf16[1,2560,5120]{2,1,0:T(8,128)(2,1)}) %all-gather.10.cloned.1.call-update) | async-done | bytes 26214416 | tf_op jit(solution)/shard_map/all_gather | solution.py:35
  762.1 23.8 %fusion = f32[640,2560]{1,0:T(8,128)} fusion(bf16[1,2560,5120]{2,1,0:T(8,128)(2,1)} %all-gather.10.cloned.1.call-done, bf16[1,1,640,5120]{3,2,1,0:T(8,128)(2,1)} %all-gather.8.cloned.1.call-done), kind=kOutput, calls=%fused_computation | convolution fusion | flops 16777216000 | bytes 39321600 | tf_op jit(solution)/shard_map/dot_general | solution.py:8
  785.9 0.0 copy-start
  785.9 0.0 copy-start.1
  785.9 0.0 all-reduce.2.cloned.1.call-update
  785.9 0.0 all-gather.6.cloned.1.call-start
  786.0 0.6 copy-done
  786.6 0.1 reshape.16
  786.8 0.1 reshape.17
  786.8 0.1 dynamic_slice.33
  786.9 0.0 copy-done.1
  786.9 0.7 fusion.3
  788.9 0.1 dynamic-slice_subtract_fusion
  789.0 29.6 %all-reduce.2.cloned.1.call-done = f32[640,2560]{1,0:T(8,128)} async-done(((f32[640,2560]{1,0:T(8,128)}), f32[640,2560]{1,0:T(8,128)}) %all-reduce.2.cloned.1.call-update) | async-done | bytes 6553616 | tf_op jit(solution)/shard_map/psum | solution.py:36
  818.6 3.6 divide_convert_fusion
  822.2 0.0 all-gather.6.cloned.1.call-update
  822.2 0.3 reduce-scatter.2.cloned.1.call-start
  822.5 183.9 %all-gather.6.cloned.1.call-done = bf16[5120,1280]{1,0:T(8,128)(2,1)} async-done(((bf16[640,1280]{1,0:T(8,128)(2,1)}), bf16[5120,1280]{1,0:T(8,128)(2,1)}) %all-gather.6.cloned.1.call-update) | async-done | bytes 13107216 | tf_op jit(solution)/shard_map/all_gather | solution.py:40
  1006.4 15.0 %fusion.5 = f32[640,5120]{1,0:T(8,128)} fusion(bf16[640,1280]{1,0:T(8,128)(2,1)} %divide_convert_fusion, bf16[5120,1280]{1,0:T(8,128)(2,1)} %all-gather.6.cloned.1.call-done), kind=kOutput, calls=%fused_computation.11 | convolution fusion | flops 8388608000 | bytes 27852800 | tf_op jit(solution)/shard_map/dot_general | solution.py:8
  1021.4 0.0 reduce-scatter.2.cloned.1.call-update
  1021.4 100.8 %reduce-scatter.2.cloned.1.call-done = f32[640,1280]{1,0:T(8,128)} async-done(((f32[640,5120]{1,0:T(8,128)}), f32[640,1280]{1,0:T(8,128)}) %reduce-scatter.2.cloned.1.call-update) | async-done | bytes 3276816 | tf_op jit(solution)/shard_map/reduce_scatter | solution.py:41
  (1 shorter events, 0.0 us)
Async XLA Ops:
  67.3 6.7 copy-start.2
  67.3 80.7 %all-to-all-start = ((bf16[2,2,819200]{2,1,0:T(2,128)(2,1)}), bf16[2,2,819200]{2,1,0:T(2,128)(2,1)}, u32[]{:S(2)}, u32[]{:S(2)}) async-start(bf16[2,2,819200]{2,1,0:T(2,128)(2,1)} %reshape.21), calls=%async_computation | async-start | bytes 13107200 | tf_op jit(solution)/shard_map/all_to_all | solution.py:29
  73.8 186.6 %all-gather.8.cloned.1.call-start = ((), (), s32[]{:S(2)}) async-start(), calls=%async_computation.5 | async-start | bytes 9830400 | tf_op jit(solution)/shard_map/all_gather | solution.py:33
  176.4 585.7 %all-gather.10.cloned.1.call-start = ((), (), s32[]{:S(2)}) async-start(), calls=%async_computation.6 | async-start | bytes 29491200 | tf_op jit(solution)/shard_map/all_gather | solution.py:35
  182.0 636.6 %all-reduce.2.cloned.1.call-start = ((), (), s32[]{:S(2)}) async-start(), calls=%async_computation.2 | async-start | bytes 13107200 | tf_op jit(solution)/shard_map/psum | solution.py:36
  785.9 0.7 copy-start
  785.9 1.0 copy-start.1
  785.9 220.5 %all-gather.6.cloned.1.call-start = ((), (), s32[]{:S(2)}) async-start(), calls=%async_computation.3 | async-start | bytes 14745600 | tf_op jit(solution)/shard_map/all_gather | solution.py:40
  822.2 300.0 %reduce-scatter.2.cloned.1.call-start = ((), (), s32[]{:S(2)}) async-start(), calls=%async_computation.4 | async-start | bytes 16384000 | tf_op jit(solution)/shard_map/reduce_scatter | solution.py:41
Sparse Core Ops, SparseCore 0:
  176.5 83.8 all-gather.7
  261.9 500.0 all-gather.9
  786.0 32.5 all-reduce.1
  822.4 183.9 all-gather.5
  1021.5 100.6 reduce-scatter.1
where the time goes:
time: 1130 us
  waiting for transfers between devices  966 us (85%)
  local copies, waits for them, and re-layouts  55.9 us (5%)
  other arithmetic  42.9 us (4%)
  matrix products  38.8 us (3%)
  between operations  18.2 us (2%)
    all_gather x1, waiting for transfers between devices, per_device(): lax.all_gather(col_piece, 'vw', axis=0, tiled=True)  502 us
    all_gather x1, waiting for transfers between devices, per_device(): lax.all_gather(amplitude, 'vw', axis=0, tiled=True)  184 us
    reduce_scatter x1, waiting for transfers between devices, per_device(): lax.psum_scatter(density_part, ('occ', 'vn'), scatter_dimension=1, tiled=...  101 us
    all_gather x1, waiting for transfers between devices, per_device(): row_tile = lax.all_gather(first_piece, 'occ', axis=0, tiled=True)  78.4 us
    all_to_all x1, waiting for transfers between devices, per_device(): lax.all_to_all(slabs, 'occ', split_axis=1, concat_axis=0, tiled=True)  71.4 us
    unnamed x11, local copies, waits for them, and re-layouts  46.8 us
    unnamed x1, other arithmetic  39.2 us
    dot_general x2, matrix products, contract_rows(): lax.dot_general(left, piece, (((1,), (1,)), ((), ())), preferred_element_...  38.8 us
  transfers between devices with their start and end apart: 6, of which 6 were waited for; matrix products, arithmetic and copies ran while one was open for 0% of the time, Pallas kernels for 0%

commit v1 on v0

v1 whole, which is shorter than its diff:
```python
import math

import jax
import jax.numpy as jnp
from jax import lax
from jax.sharding import PartitionSpec as P

CHUNKS = 2


def contract_rows(left, piece):
    return lax.dot_general(
        left, piece, (((1,), (1,)), ((), ())), preferred_element_type=jnp.float32
    )


def contract_first(left, right):
    return lax.dot_general(
        left, right, (((0,), (0,)), ((), ())), preferred_element_type=jnp.float32
    )


def pick(items, index):
    chosen = items[0]
    for position in range(1, len(items)):
        chosen = jnp.where(index == position, items[position], chosen)
    return chosen


def cuts(extent, parts):
    unit = 16 if extent % 16 == 0 and extent // 16 >= parts else 1
    marks = [extent // unit * part // parts * unit for part in range(parts + 1)]
    return [(low, high) for low, high in zip(marks, marks[1:]) if high > low]


def whole_rows(slabs, pair_list, occ_energy, virt_energy):
    n_vw = lax.axis_size("vw")
    n_occ = lax.axis_size("occ")
    n_vn = lax.axis_size("vn")
    tile_rows = slabs.shape[1]
    sub_rows = tile_rows // n_occ
    my_occ = lax.axis_index("occ")
    my_vw = lax.axis_index("vw")
    my_vn = lax.axis_index("vn")
    row_energy = lax.dynamic_slice_in_dim(virt_energy, my_vw * tile_rows, tile_rows)
    energy_grid = virt_energy.reshape(n_vw, n_occ, sub_rows)
    col_energy = lax.dynamic_index_in_dim(energy_grid, my_occ, 1, keepdims=False).reshape(
        n_vw * sub_rows
    )
    share = n_vw * sub_rows // n_vn
    col_share = lax.dynamic_slice_in_dim(col_energy, my_vn * share, share)
    pieces = lax.all_to_all(slabs, "occ", split_axis=1, concat_axis=0, tiled=True)
    density = 0.0
    for index in range(pair_list.shape[0]):
        first = pair_list[index, 0]
        second = pair_list[index, 1]
        first_piece = lax.dynamic_index_in_dim(pieces, first, 0, keepdims=False)
        row_tile = lax.all_gather(first_piece, "occ", axis=0, tiled=True)
        col_piece = lax.dynamic_index_in_dim(pieces, second, 0, keepdims=False)
        integrals = contract_rows(row_tile, lax.all_gather(col_piece, "vw", axis=0, tiled=True))
        summed = lax.psum(integrals, "vn")
        mine = lax.dynamic_slice_in_dim(summed, my_vn * share, share, 1)
        denom = occ_energy[first] + occ_energy[second] - row_energy[:, None] - col_share[None, :]
        amplitude = (mine / denom).astype(jnp.bfloat16)
        density += contract_rows(amplitude, lax.all_gather(amplitude, "vw", axis=0, tiled=True))
    return lax.psum_scatter(density, ("occ", "vn"), scatter_dimension=1, tiled=True)


def grid_blocks(slabs, pair_list, occ_energy, virt_energy):
    n_vw, n_occ, n_vn = (lax.axis_size(name) for name in ("vw", "occ", "vn"))
    side = math.isqrt(n_occ * n_vn)
    depth = n_vw // (side * side)
    group = side // n_vn
    held, tile, k_dev = slabs.shape
    sub = tile // n_occ
    k_part = k_dev // n_occ
    x, w, v = (lax.axis_index(name) for name in ("occ", "vw", "vn"))
    r, s, y = w // (side * depth), w // depth % side, w % depth

    def at(row, col, deep):
        return (row % side * side + col % side) * depth + deep % depth

    places = [(a, b, c) for a in range(side) for b in range(side) for c in range(depth)]

    def send_vw(array, target):
        pairs = [(at(*place), at(*target(*place))) for place in places]
        if all(source == goal for source, goal in pairs):
            return array
        return lax.ppermute(array, "vw", pairs)

    def send_on(array, axis, extent, step):
        return lax.ppermute(array, axis, [(a, (a + step) % extent) for a in range(extent)])

    rows_by_sub = slabs.reshape(held, n_occ, sub, k_dev)
    energy = virt_energy.reshape(n_vw, n_occ, sub)
    chunks = cuts(sub, CHUNKS)

    shares = []
    for low, high in chunks:
        rows = rows_by_sub[:, :, low:high]
        parts = [
            lax.dynamic_slice_in_dim(rows, (x + step) % n_occ * k_part, k_part, 3)
            for step in range(n_occ)
        ]
        shares.append(
            [parts[0]] + [send_on(parts[step], "occ", n_occ, step) for step in range(1, n_occ)]
        )

    def orbital_rows(share, orbital):
        mine = [lax.dynamic_index_in_dim(part, orbital % held, 0, keepdims=False) for part in share]
        return pick(mine, (x - orbital // held) % n_occ)

    total = 0.0
    for index in range(pair_list.shape[0]):
        first, second = pair_list[index, 0], pair_list[index, 1]
        row_shares = [orbital_rows(share, first) for share in shares]
        col_shares = [
            jnp.roll(orbital_rows(share, second), -x, 0) for share in shares
        ]
        row_parts = [
            [part] + [send_vw(part, lambda a, b, c, d=d: (a, b - d, c)) for d in range(1, side)]
            for part in row_shares
        ]
        tiles = [
            jnp.concatenate([part[d] for part in row_parts], 1).reshape(tile, k_part)
            for d in range(side)
        ]
        row_sets = []
        for step in range(n_vn):
            core = (v + step) % n_vn
            row_sets.append(
                jnp.concatenate(
                    [pick(tiles, (q * n_vn + core - s) % side) for q in range(group)], 0
                )
            )
        row_index = [at(r, q * n_vn + v, y) for q in range(group)]
        row_energy = jnp.concatenate(
            [lax.dynamic_index_in_dim(energy, i, 0, keepdims=False).reshape(tile) for i in row_index]
        )
        pair_energy = occ_energy[first] + occ_energy[second]

        amplitude = []
        for d in range(side):
            amplitude.append([])
            for part, (low, high) in zip(col_shares, chunks):
                arrived = send_vw(part, lambda a, b, c, d=d: (b - d, a, c))
                columns = [arrived] + [
                    send_vw(arrived, lambda a, b, c, l=l: (a, b, c - l)) for l in range(1, depth)
                ]
                size = depth * (high - low)
                sums = []
                for step in range(n_occ):
                    these = jnp.stack([col[step] for col in columns]).reshape(size, k_part)
                    sums.append([contract_rows(these, rows) for rows in row_sets])
                done = []
                for partial in sums:
                    kept = partial[0]
                    for step in range(1, n_vn):
                        kept = kept + send_on(partial[step], "vn", n_vn, step)
                    done.append(kept)
                integrals = done[0]
                for step in range(1, n_occ):
                    integrals = integrals + send_on(done[step], "occ", n_occ, step)
                col_energy = jnp.concatenate(
                    [
                        lax.dynamic_slice(
                            energy, (at(s, r + d, y + l), x, low), (1, 1, high - low)
                        ).reshape(high - low)
                        for l in range(depth)
                    ]
                )
                denom = pair_energy - row_energy[None, :] - col_energy[:, None]
                block = (integrals / denom).astype(jnp.bfloat16)
                amplitude[d].append(block.reshape(depth, high - low, block.shape[1]))

        def in_order(blocks, row, deep):
            ordered = []
            for a in range(side):
                by_tile = [
                    pick([blocks[d][h] for d in range(side)], (a - row) % side)
                    for h in range(len(chunks))
                ]
                for b in range(depth):
                    ordered += [
                        pick([part[l] for l in range(depth)], (b - deep) % depth)
                        for part in by_tile
                    ]
            return jnp.concatenate(ordered, 0)

        gathered = {}
        for a in range(side):
            for c in range(depth):
                if a == 0 and c == 0:
                    gathered[a, c] = in_order(amplitude, r, y)
                elif c == 0:
                    gathered[a, c] = send_vw(
                        gathered[0, 0], lambda i, j, k, a=a: (i - a, j, k)
                    )
                else:
                    gathered[a, c] = send_vw(
                        gathered[a, 0], lambda i, j, k, c=c: (i, j, k - c)
                    )
        cores = [gathered[0, 0]] + [
            send_on(gathered[0, 0], "vn", n_vn, n_vn - step) for step in range(1, n_vn)
        ]
        count = gathered[0, 0].shape[0]
        by_s = [
            pick([core.reshape(count, group, tile)[:, q] for core in cores], (b - v) % n_vn)
            for q in range(group)
            for b in range(n_vn)
        ]
        left = [pick(by_s, (s + d) % side) for d in range(side)]

        def right(step, deep):
            goal = (x + step) % n_occ
            split = [gathered[a, deep].reshape(count, group, tile) for a in range(side)]
            options = [split[(a)][:, q] for a in range(side) for q in range(group)]
            return pick(options, (goal // group - r) % side * group + goal % group)

        parts = []
        for deep in range(depth):
            rights = [right(step, deep) for step in range(n_occ)]
            terms = [[contract_first(rows, cols) for cols in rights] for rows in left]
            if deep % 2 == 0:
                by_row = []
                for row in terms:
                    kept = row[0]
                    for step in range(1, n_occ):
                        kept = kept + send_on(
                            row[step].astype(jnp.bfloat16), "occ", n_occ, step
                        ).astype(jnp.float32)
                    by_row.append(kept)
                kept = by_row[0]
                for d in range(1, side):
                    kept = kept + send_vw(
                        by_row[d].astype(jnp.bfloat16), lambda i, j, k, d=d: (i, j + d, k)
                    ).astype(jnp.float32)
            else:
                by_col = []
                for step in range(n_occ):
                    kept = terms[0][step]
                    for d in range(1, side):
                        kept = kept + send_vw(
                            terms[d][step].astype(jnp.bfloat16),
                            lambda i, j, k, d=d: (i, j + d, k),
                        ).astype(jnp.float32)
                    by_col.append(kept)
                kept = by_col[0]
                for step in range(1, n_occ):
                    kept = kept + send_on(
                        by_col[step].astype(jnp.bfloat16), "occ", n_occ, step
                    ).astype(jnp.float32)
            parts.append(kept)
        ordered = [pick(parts, (c - y) % depth) for c in range(depth)]
        total = total + jnp.concatenate(ordered, 1)
    return total


def solution(mesh):
    in_specs = (P("occ", "vw", "vn"), P(), P(), P())
    out_specs = P("vw", ("occ", "vn"))
    n_occ, n_vw, n_vn = (mesh.shape[name] for name in ("occ", "vw", "vn"))
    side = math.isqrt(n_occ * n_vn)
    fits = side * side == n_occ * n_vn and n_vw % (side * side) == 0 and side % n_vn == 0
    return jax.shard_map(
        grid_blocks if fits else whole_rows,
        mesh=mesh,
        in_specs=in_specs,
        out_specs=out_specs,
        check_vma=False,
    )
```

time: 1130 us -> 526 us (0.47)
  waiting for transfers between devices: 966 us -> 407 us
  local copies, waits for them, and re-layouts: 55.9 us -> 14.7 us
  other arithmetic: 42.9 us -> 11.1 us
  starting transfers between devices: 7.09 us -> 35.2 us
    all_gather x3 -> x0, waiting for transfers between devices: 764 us -> none  [the longest x1 502 us: per_device(): lax.all_gather(col_piece, 'vw', axis=0, tiled=True)]
    ppermute x0 -> x34, waiting for transfers between devices: none -> 407 us  [the longest x16 292 us: send_vw(): return lax.ppermute(array, 'vw', pairs)]
    reduce_scatter x1 -> x0, waiting for transfers between devices: 101 us -> none  [per_device(): lax.psum_scatter(density_part, ('occ', 'vn'), scatter_dimension=1, tiled=...]
    all_to_all x1 -> x0, waiting for transfers between devices: 71.4 us -> none  [per_device(): lax.all_to_all(slabs, 'occ', split_axis=1, concat_axis=0, tiled=True)]
    unnamed x11, local copies, waits for them, and re-layouts: 46.8 us -> 0.13 us
    unnamed x1 -> x7, other arithmetic: 39.2 us -> 0.44 us
    ppermute x0 -> x34, starting transfers between devices: none -> 35.2 us  [the longest x16 24.4 us: send_vw(): return lax.ppermute(array, 'vw', pairs)]
    psum x1 -> x0, waiting for transfers between devices: 29.6 us -> none  [per_device(): summed = lax.psum(integrals, 'vn')]
  transfers between devices with their start and end apart: 6 -> 34, of which waited for: 6 -> 17; matrix products, arithmetic and copies ran while one was open for 0% -> 10% of each run, Pallas kernels for 0% -> 0%
where the time goes in v1:
time: 526 us; the launch traced here: 521 us
  waiting for transfers between devices  407 us (77%)
  matrix products  45 us (9%)
  starting transfers between devices  35.2 us (7%)
  local copies, waits for them, and re-layouts  14.7 us (3%)
  other arithmetic  11.1 us (2%)
  between operations  7.79 us (1%)
    ppermute x16, waiting for transfers between devices, send_vw(): return lax.ppermute(array, 'vw', pairs)  292 us
    ppermute x18, waiting for transfers between devices, send_on(): lax.ppermute(array, axis, [(a, (a + step) % extent) for a in range(extent)])  116 us
    ppermute x16, starting transfers between devices, send_vw(): return lax.ppermute(array, 'vw', pairs)  24.4 us
    dot_general x16, matrix products, contract_rows(): lax.dot_general(left, piece, (((1,), (1,)), ((), ())), preferred_element_...  23.8 us
    dot_general x8, matrix products, contract_first(): lax.dot_general(left, right, (((0,), (0,)), ((), ())), preferred_element_...  21.2 us
    ppermute x18, starting transfers between devices, send_on(): lax.ppermute(array, axis, [(a, (a + step) % extent) for a in range(extent)])  10.8 us
  transfers between devices with their start and end apart: 34, of which 17 were waited for; matrix products, arithmetic and copies ran while one was open for 10% of the time, Pallas kernels for 0%

profile of v1, /device:TPU:0, one launch (start us, length us, event | category | flops | bytes accessed | tf_op | source)
XLA Modules:
  0.0 521.1 jit_solution(9323925460348598675)
XLA Ops:
  0.0 5.1 fusion.16
  5.1 2.7 constant_dynamic-slice_fusion.5
  7.8 2.9 collective-permute-start.4
  20.3 27.4 %collective-permute-done.4 = bf16[1,2,160,2560]{3,2,1,0:T(8,128)(2,1)} collective-permute-done((bf16[1,2,160,2560]{3,2,1,0:T(8,128)(2,1)}, bf16[1,2,160,2560]{3,2,1,0:T(8,128)(2,1)}, u32[]{:S(2)}, u32[]{:S(2)}) %collective-permute-start.4) | collective-permute-done | bytes 1638432 | tf_op jit(solution)/shard_map/ppermute | solution.py:92
  47.7 2.5 select_bitcast_fusion
  50.8 3.2 collective-permute-start.14
  54.7 27.2 %collective-permute-done = bf16[1,2,160,2560]{3,2,1,0:T(8,128)(2,1)} collective-permute-done((bf16[1,2,160,2560]{3,2,1,0:T(8,128)(2,1)}, bf16[1,2,160,2560]{3,2,1,0:T(8,128)(2,1)}, u32[]{:S(2)}, u32[]{:S(2)}) %collective-permute-start) | collective-permute-done | bytes 1638432 | tf_op jit(solution)/shard_map/ppermute | solution.py:92
  82.0 2.0 select_bitcast_fusion.2
  84.0 1.9 collective-permute-start.3
  86.5 2.6 collective-permute-start.1
  90.3 2.2 collective-permute-start.5
  92.5 31.7 %collective-permute-done.3 = bf16[2,160,2560]{2,1,0:T(8,128)(2,1)S(1)} collective-permute-done((bf16[2,160,2560]{2,1,0:T(8,128)(2,1)S(1)}, bf16[2,160,2560]{2,1,0:T(8,128)(2,1)S(1)}, u32[]{:S(2)}, u32[]{:S(2)}) %collective-permute-start.3) | collective-permute-done | bytes 1638432 | tf_op jit(solution)/shard_map/ppermute | solution.py:89
  124.2 1.5 collective-permute-start.15
  126.4 32.9 %collective-permute-done.1 = bf16[2,160,2560]{2,1,0:T(8,128)(2,1)S(1)} collective-permute-done((bf16[2,160,2560]{2,1,0:T(8,128)(2,1)S(1)}, bf16[2,160,2560]{2,1,0:T(8,128)(2,1)S(1)}, u32[]{:S(2)}, u32[]{:S(2)}) %collective-permute-start.1) | collective-permute-done | bytes 1638432 | tf_op jit(solution)/shard_map/ppermute | solution.py:89
  159.4 1.5 collective-permute-start.2
  161.6 30.8 %collective-permute-done.5 = bf16[2,160,2560]{2,1,0:T(8,128)(2,1)S(1)} collective-permute-done((bf16[2,160,2560]{2,1,0:T(8,128)(2,1)S(1)}, bf16[2,160,2560]{2,1,0:T(8,128)(2,1)S(1)}, u32[]{:S(2)}, u32[]{:S(2)}) %collective-permute-start.5) | collective-permute-done | bytes 1638432 | tf_op jit(solution)/shard_map/ppermute | solution.py:89
  194.3 1.5 fusion.31
  199.9 33.3 %collective-permute-done.2 = bf16[2,160,2560]{2,1,0:T(8,128)(2,1)S(1)} collective-permute-done((bf16[2,160,2560]{2,1,0:T(8,128)(2,1)S(1)}, bf16[2,160,2560]{2,1,0:T(8,128)(2,1)S(1)}, u32[]{:S(2)}, u32[]{:S(2)}) %collective-permute-start.2) | collective-permute-done | bytes 1638432 | tf_op jit(solution)/shard_map/ppermute | solution.py:89
  238.2 26.0 %collective-permute-done.10 = bf16[2,160,2560]{2,1,0:T(8,128)(2,1)S(1)} collective-permute-done((bf16[2,160,2560]{2,1,0:T(8,128)(2,1)S(1)}, bf16[2,160,2560]{2,1,0:T(8,128)(2,1)S(1)}, u32[]{:S(2)}, u32[]{:S(2)}) %collective-permute-start.10) | collective-permute-done | bytes 1638432 | tf_op jit(solution)/shard_map/ppermute | solution.py:89
  268.3 1.5 convolution_add_fusion.2
  269.8 1.5 convolution_add_fusion.4
  272.7 1.5 convolution_add_fusion.6
  274.9 1.7 convolution_add_fusion
  276.7 15.7 %collective-permute-done.13 = f32[320,640]{1,0:T(8,128)S(1)} collective-permute-done((f32[320,640]{1,0:T(8,128)S(1)}, f32[320,640]{1,0:T(8,128)S(1)}, u32[]{:S(2)}, u32[]{:S(2)}) %collective-permute-start.13) | collective-permute-done | bytes 819232 | tf_op jit(solution)/shard_map/ppermute | solution.py:92
  293.8 1.5 fusion.9
  296.0 14.0 %collective-permute-done.8 = f32[320,640]{1,0:T(8,128)S(1)} collective-permute-done((f32[320,640]{1,0:T(8,128)S(1)}, f32[320,640]{1,0:T(8,128)S(1)}, u32[]{:S(2)}, u32[]{:S(2)}) %collective-permute-start.8) | collective-permute-done | bytes 819232 | tf_op jit(solution)/shard_map/ppermute | solution.py:92
  310.0 1.5 broadcast_select_fusion.21
  311.6 15.9 %collective-permute-done.23 = f32[320,640]{1,0:T(8,128)S(1)} collective-permute-done((f32[320,640]{1,0:T(8,128)S(1)}, f32[320,640]{1,0:T(8,128)S(1)}, u32[]{:S(2)}, u32[]{:S(2)}) %collective-permute-start.23) | collective-permute-done | bytes 819232 | tf_op jit(solution)/shard_map/ppermute | solution.py:92
  327.5 1.5 fusion.13
  329.0 15.7 %collective-permute-done.18 = f32[320,640]{1,0:T(8,128)S(1)} collective-permute-done((f32[320,640]{1,0:T(8,128)S(1)}, f32[320,640]{1,0:T(8,128)S(1)}, u32[]{:S(2)}, u32[]{:S(2)}) %collective-permute-start.18) | collective-permute-done | bytes 819232 | tf_op jit(solution)/shard_map/ppermute | solution.py:92
  344.7 1.6 broadcast_select_fusion.20
  346.7 2.4 collective-permute-start.25
  349.1 1.5 collective-permute-start.27
  350.7 69.7 %collective-permute-done.25 = bf16[1280,640]{1,0:T(8,128)(2,1)} collective-permute-done((bf16[1280,640]{1,0:T(8,128)(2,1)S(1)}, bf16[1280,640]{1,0:T(8,128)(2,1)}, u32[]{:S(2)}, u32[]{:S(2)}) %collective-permute-start.25) | collective-permute-done | bytes 1638432 | tf_op jit(solution)/shard_map/ppermute | solution.py:89
  421.8 1.9 broadcast_select_fusion.9
  423.6 2.9 convolution_convert_fusion
  426.7 3.0 convolution_convert_fusion.1
  430.3 27.1 %collective-permute-done.26 = bf16[1280,640]{1,0:T(8,128)(2,1)} collective-permute-done((bf16[1280,640]{1,0:T(8,128)(2,1)}, bf16[1280,640]{1,0:T(8,128)(2,1)}, u32[]{:S(2)}, u32[]{:S(2)}) %collective-permute-start.26) | collective-permute-done | bytes 1638432 | tf_op jit(solution)/shard_map/ppermute | solution.py:89
  457.4 2.9 convolution_convert_fusion.2
  461.7 1.8 add_convert_fusion
  464.2 2.9 convolution_convert_fusion.3
  468.6 13.0 %collective-permute-done.29 = bf16[640,640]{0,1:T(8,128)(2,1)S(1)} collective-permute-done((bf16[640,640]{0,1:T(8,128)(2,1)S(1)}, bf16[640,640]{0,1:T(8,128)(2,1)S(1)}, u32[]{:S(2)}, u32[]{:S(2)}) %collective-permute-start.29) | collective-permute-done | bytes 819232 | tf_op jit(solution)/shard_map/ppermute | solution.py:89
  481.6 2.9 add_convert_fusion.1
  485.8 1.6 fusion.14
  487.4 11.7 %collective-permute-done.33 = bf16[640,640]{0,1:T(8,128)(2,1)S(1)} collective-permute-done((bf16[640,640]{0,1:T(8,128)(2,1)S(1)}, bf16[640,640]{0,1:T(8,128)(2,1)S(1)}, u32[]{:S(2)}, u32[]{:S(2)}) %collective-permute-start.33) | collective-permute-done | bytes 819232 | tf_op jit(solution)/shard_map/ppermute | solution.py:89
  499.1 15.3 %collective-permute-done.28 = bf16[640,640]{0,1:T(8,128)(2,1)S(1)} collective-permute-done((bf16[640,640]{0,1:T(8,128)(2,1)S(1)}, bf16[640,640]{0,1:T(8,128)(2,1)S(1)}, u32[]{:S(2)}, u32[]{:S(2)}) %collective-permute-start.28) | collective-permute-done | bytes 819232 | tf_op jit(solution)/shard_map/ppermute | solution.py:89
  514.4 3.1 broadcast_select_fusion.11
  517.7 3.0 copy.11
  (101 shorter events, 34.3 us)
Async XLA Ops:
  7.8 39.9 %collective-permute-start.4 = (bf16[1,2,160,2560]{3,2,1,0:T(8,128)(2,1)}, bf16[1,2,160,2560]{3,2,1,0:T(8,128)(2,1)}, u32[]{:S(2)}, u32[]{:S(2)}) collective-permute-start(bf16[1,2,160,2560]{3,2,1,0:T(8,128)(2,1)} %constant_dynamic-slice_fusion.5), channel_id=1, source_target_pairs={{0,16},{16,0},{1,17},{17,1},{2,18},{18,2},{3,19},{19,3},{4,20},{20... | collective-permute-start | bytes 4915208 | tf_op jit(solution)/shard_map/ppermute | solution.py:92
  10.7 1.3 copy-start.4
  10.7 6.1 %copy-start.2 = (f32[5120]{0:T(1024)S(1)}, f32[5120]{0:T(1024)}, u32[]{:S(2)}) copy-start(f32[5120]{0:T(1024)} %param.9) | copy-start | bytes 61444
  10.7 7.5 %copy-start.3 = (f32[2]{0:T(128)S(1)}, f32[2]{0:T(128)}, u32[]{:S(2)}) copy-start(f32[2]{0:T(128)} %param.8) | copy-start | bytes 28
  12.1 69.9 %collective-permute-start = (bf16[1,2,160,2560]{3,2,1,0:T(8,128)(2,1)}, bf16[1,2,160,2560]{3,2,1,0:T(8,128)(2,1)}, u32[]{:S(2)}, u32[]{:S(2)}) collective-permute-start(bf16[1,2,160,2560]{3,2,1,0:T(8,128)(2,1)} %constant_dynamic-slice_fusion.6), channel_id=1, source_target_pairs={{0,16},{16,0},{1,17},{17,1},{2,18},{18,2},{3,19},{19,3},{4,20},{20... | collective-permute-start | bytes 4915208 | tf_op jit(solution)/shard_map/ppermute | solution.py:92
  50.8 39.5 %collective-permute-start.14 = (bf16[2,160,2560]{2,1,0:T(8,128)(2,1)S(1)}, bf16[2,160,2560]{2,1,0:T(8,128)(2,1)S(1)}, u32[]{:S(2)}, u32[]{:S(2)}) collective-permute-start(bf16[2,160,2560]{2,1,0:T(8,128)(2,1)S(1)} %fusion), channel_id=1, source_target_pairs={{0,8},{2,10},{4,0},{6,2},{8,12},{10,14},{12,4},{14,6},{1,9},{3,11}... | collective-permute-start | bytes 4915208 | tf_op jit(solution)/shard_map/ppermute | solution.py:89
  54.0 71.9 %collective-permute-start.19 = (bf16[2,160,2560]{2,1,0:T(8,128)(2,1)S(1)}, bf16[2,160,2560]{2,1,0:T(8,128)(2,1)S(1)}, u32[]{:S(2)}, u32[]{:S(2)}) collective-permute-start(bf16[2,160,2560]{2,1,0:T(8,128)(2,1)S(1)} %fusion), channel_id=1, source_target_pairs={{0,0},{2,2},{4,8},{6,10},{8,4},{10,6},{12,12},{14,14},{1,1},{3,3},... | collective-permute-start | bytes 4915208 | tf_op jit(solution)/shard_map/ppermute | solution.py:89
  84.0 40.2 %collective-permute-start.3 = (bf16[2,160,2560]{2,1,0:T(8,128)(2,1)S(1)}, bf16[2,160,2560]{2,1,0:T(8,128)(2,1)S(1)}, u32[]{:S(2)}, u32[]{:S(2)}) collective-permute-start(bf16[2,160,2560]{2,1,0:T(8,128)(2,1)S(1)} %get-tuple-element.14), channel_id=1, source_target_pairs={{0,4},{2,6},{4,0},{6,2},{8,12},{10,14},{12,8},{14,10},{1,5},{3,7},... | collective-permute-start | bytes 4915208 | tf_op jit(solution)/shard_map/ppermute | solution.py:89
  86.5 72.9 %collective-permute-start.1 = (bf16[2,160,2560]{2,1,0:T(8,128)(2,1)S(1)}, bf16[2,160,2560]{2,1,0:T(8,128)(2,1)S(1)}, u32[]{:S(2)}, u32[]{:S(2)}) collective-permute-start(bf16[2,160,2560]{2,1,0:T(8,128)(2,1)S(1)} %fusion.1), channel_id=1, source_target_pairs={{0,8},{2,10},{4,0},{6,2},{8,12},{10,14},{12,4},{14,6},{1,9},{3,11}... | collective-permute-start | bytes 4915208 | tf_op jit(solution)/shard_map/ppermute | solution.py:89
  89.1 71.8 %collective-permute-start.9 = (bf16[2,160,2560]{2,1,0:T(8,128)(2,1)S(1)}, bf16[2,160,2560]{2,1,0:T(8,128)(2,1)S(1)}, u32[]{:S(2)}, u32[]{:S(2)}) collective-permute-start(bf16[2,160,2560]{2,1,0:T(8,128)(2,1)S(1)} %fusion.1), channel_id=1, source_target_pairs={{0,0},{2,2},{4,8},{6,10},{8,4},{10,6},{12,12},{14,14},{1,1},{3,3},... | collective-permute-start | bytes 4915208 | tf_op jit(solution)/shard_map/ppermute | solution.py:89
  90.3 102.2 %collective-permute-start.5 = (bf16[2,160,2560]{2,1,0:T(8,128)(2,1)S(1)}, bf16[2,160,2560]{2,1,0:T(8,128)(2,1)S(1)}, u32[]{:S(2)}, u32[]{:S(2)}) collective-permute-start(bf16[2,160,2560]{2,1,0:T(8,128)(2,1)S(1)} %get-tuple-element.13), channel_id=1, source_target_pairs={{0,4},{2,6},{4,0},{6,2},{8,12},{10,14},{12,8},{14,10},{1,5},{3,7},... | collective-permute-start | bytes 4915208 | tf_op jit(solution)/shard_map/ppermute | solution.py:89
  124.2 69.8 %collective-permute-start.15 = (bf16[2,160,2560]{2,1,0:T(8,128)(2,1)S(1)}, bf16[2,160,2560]{2,1,0:T(8,128)(2,1)S(1)}, u32[]{:S(2)}, u32[]{:S(2)}) collective-permute-start(bf16[2,160,2560]{2,1,0:T(8,128)(2,1)S(1)} %collective-permute-done.14), channel_id=1, source_target_pairs={{0,2},{2,0},{4,6},{6,4},{8,10},{10,8},{12,14},{14,12},{1,3},{3,1},... | collective-permute-start | bytes 4915208 | tf_op jit(solution)/shard_map/ppermute | solution.py:89
  125.9 72.2 %collective-permute-start.20 = (bf16[2,160,2560]{2,1,0:T(8,128)(2,1)S(1)}, bf16[2,160,2560]{2,1,0:T(8,128)(2,1)S(1)}, u32[]{:S(2)}, u32[]{:S(2)}) collective-permute-start(bf16[2,160,2560]{2,1,0:T(8,128)(2,1)S(1)} %collective-permute-done.19), channel_id=1, source_target_pairs={{0,2},{2,0},{4,6},{6,4},{8,10},{10,8},{12,14},{14,12},{1,3},{3,1},... | collective-permute-start | bytes 4915208 | tf_op jit(solution)/shard_map/ppermute | solution.py:89
  159.4 73.8 %collective-permute-start.2 = (bf16[2,160,2560]{2,1,0:T(8,128)(2,1)S(1)}, bf16[2,160,2560]{2,1,0:T(8,128)(2,1)S(1)}, u32[]{:S(2)}, u32[]{:S(2)}) collective-permute-start(bf16[2,160,2560]{2,1,0:T(8,128)(2,1)S(1)} %collective-permute-done.1), channel_id=1, source_target_pairs={{0,2},{2,0},{4,6},{6,4},{8,10},{10,8},{12,14},{14,12},{1,3},{3,1},... | collective-permute-start | bytes 4915208 | tf_op jit(solution)/shard_map/ppermute | solution.py:89
  160.9 103.3 %collective-permute-start.10 = (bf16[2,160,2560]{2,1,0:T(8,128)(2,1)S(1)}, bf16[2,160,2560]{2,1,0:T(8,128)(2,1)S(1)}, u32[]{:S(2)}, u32[]{:S(2)}) collective-permute-start(bf16[2,160,2560]{2,1,0:T(8,128)(2,1)S(1)} %collective-permute-done.9), channel_id=1, source_target_pairs={{0,2},{2,0},{4,6},{6,4},{8,10},{10,8},{12,14},{14,12},{1,3},{3,1},... | collective-permute-start | bytes 4915208 | tf_op jit(solution)/shard_map/ppermute | solution.py:89
  195.7 133.3 %collective-permute-start.16 = (f32[320,640]{1,0:T(8,128)S(1)}, f32[320,640]{1,0:T(8,128)S(1)}, u32[]{:S(2)}, u32[]{:S(2)}) collective-permute-start(f32[320,640]{1,0:T(8,128)S(1)} %fusion.31), channel_id=1, source_target_pairs={{0,1},{1,0},{2,3},{3,2},{4,5},{5,4},{6,7},{7,6},{8,9},{9,8},{10,11... | collective-permute-start | bytes 2457608 | tf_op jit(solution)/shard_map/ppermute | solution.py:92
  197.4 70.2 %collective-permute-start.17 = (f32[320,640]{1,0:T(8,128)S(1)}, f32[320,640]{1,0:T(8,128)S(1)}, u32[]{:S(2)}, u32[]{:S(2)}) collective-permute-start(f32[320,640]{1,0:T(8,128)S(1)} %fusion.32), channel_id=1, source_target_pairs={{0,1},{1,0},{2,3},{3,2},{4,5},{5,4},{6,7},{7,6},{8,9},{9,8},{10,11... | collective-permute-start | bytes 2457608 | tf_op jit(solution)/shard_map/ppermute | solution.py:92
  199.8 74.4 %collective-permute-start.22 = (f32[320,640]{1,0:T(8,128)S(1)}, f32[320,640]{1,0:T(8,128)S(1)}, u32[]{:S(2)}, u32[]{:S(2)}) collective-permute-start(f32[320,640]{1,0:T(8,128)S(1)} %fusion.34), channel_id=1, source_target_pairs={{0,1},{1,0},{2,3},{3,2},{4,5},{5,4},{6,7},{7,6},{8,9},{9,8},{10,11... | collective-permute-start | bytes 2457608 | tf_op jit(solution)/shard_map/ppermute | solution.py:92
  234.9 60.3 %collective-permute-start.6 = (f32[320,640]{1,0:T(8,128)S(1)}, f32[320,640]{1,0:T(8,128)S(1)}, u32[]{:S(2)}, u32[]{:S(2)}) collective-permute-start(f32[320,640]{1,0:T(8,128)S(1)} %fusion.27), channel_id=1, source_target_pairs={{0,1},{1,0},{2,3},{3,2},{4,5},{5,4},{6,7},{7,6},{8,9},{9,8},{10,11... | collective-permute-start | bytes 2457608 | tf_op jit(solution)/shard_map/ppermute | solution.py:92
  266.0 3.8 collective-permute-start.12
  267.7 3.6 collective-permute-start.7
  269.7 6.9 %collective-permute-start.11 = (f32[320,640]{1,0:T(8,128)S(1)}, f32[320,640]{1,0:T(8,128)S(1)}, u32[]{:S(2)}, u32[]{:S(2)}) collective-permute-start(f32[320,640]{1,0:T(8,128)S(1)} %fusion.29), channel_id=1, source_target_pairs={{0,1},{1,0},{2,3},{3,2},{4,5},{5,4},{6,7},{7,6},{8,9},{9,8},{10,11... | collective-permute-start | bytes 2457608 | tf_op jit(solution)/shard_map/ppermute | solution.py:92
  271.3 21.1 %collective-permute-start.13 = (f32[320,640]{1,0:T(8,128)S(1)}, f32[320,640]{1,0:T(8,128)S(1)}, u32[]{:S(2)}, u32[]{:S(2)}) collective-permute-start(f32[320,640]{1,0:T(8,128)S(1)} %convolution_add_fusion.4), channel_id=1, source_target_pairs={{0,16},{16,0},{1,17},{17,1},{2,18},{18,2},{3,19},{19,3},{4,20},{20... | collective-permute-start | bytes 2457608 | tf_op jit(solution)/shard_map/ppermute | solution.py:92
  274.2 35.8 %collective-permute-start.8 = (f32[320,640]{1,0:T(8,128)S(1)}, f32[320,640]{1,0:T(8,128)S(1)}, u32[]{:S(2)}, u32[]{:S(2)}) collective-permute-start(f32[320,640]{1,0:T(8,128)S(1)} %convolution_add_fusion.6), channel_id=1, source_target_pairs={{0,16},{16,0},{1,17},{17,1},{2,18},{18,2},{3,19},{19,3},{4,20},{20... | collective-permute-start | bytes 2457608 | tf_op jit(solution)/shard_map/ppermute | solution.py:92
  276.6 34.9 %collective-permute-start.21 = (f32[320,640]{1,0:T(8,128)S(1)}, f32[320,640]{1,0:T(8,128)S(1)}, u32[]{:S(2)}, u32[]{:S(2)}) collective-permute-start(f32[320,640]{1,0:T(8,128)S(1)} %fusion.33), channel_id=1, source_target_pairs={{0,1},{1,0},{2,3},{3,2},{4,5},{5,4},{6,7},{7,6},{8,9},{9,8},{10,11... | collective-permute-start | bytes 2457608 | tf_op jit(solution)/shard_map/ppermute | solution.py:92
  292.4 35.1 %collective-permute-start.23 = (f32[320,640]{1,0:T(8,128)S(1)}, f32[320,640]{1,0:T(8,128)S(1)}, u32[]{:S(2)}, u32[]{:S(2)}) collective-permute-start(f32[320,640]{1,0:T(8,128)S(1)} %convolution_add_fusion), channel_id=1, source_target_pairs={{0,16},{16,0},{1,17},{17,1},{2,18},{18,2},{3,19},{19,3},{4,20},{20... | collective-permute-start | bytes 2457608 | tf_op jit(solution)/shard_map/ppermute | solution.py:92
  295.3 49.4 %collective-permute-start.18 = (f32[320,640]{1,0:T(8,128)S(1)}, f32[320,640]{1,0:T(8,128)S(1)}, u32[]{:S(2)}, u32[]{:S(2)}) collective-permute-start(f32[320,640]{1,0:T(8,128)S(1)} %convolution_add_fusion.2), channel_id=1, source_target_pairs={{0,16},{16,0},{1,17},{17,1},{2,18},{18,2},{3,19},{19,3},{4,20},{20... | collective-permute-start | bytes 2457608 | tf_op jit(solution)/shard_map/ppermute | solution.py:92
  346.7 115.0 %copy-start = (bf16[1280,640]{1,0:T(8,128)(2,1)}, bf16[1280,640]{1,0:T(8,128)(2,1)S(1)}, u32[]{:S(2)}) copy-start(bf16[1280,640]{1,0:T(8,128)(2,1)S(1)} %select_dynamic-update-slice_fusion) | copy-start | bytes 4915204
  346.7 73.6 %collective-permute-start.25 = (bf16[1280,640]{1,0:T(8,128)(2,1)S(1)}, bf16[1280,640]{1,0:T(8,128)(2,1)}, u32[]{:S(2)}, u32[]{:S(2)}) collective-permute-start(bf16[1280,640]{1,0:T(8,128)(2,1)S(1)} %select_dynamic-update-slice_fusion), channel_id=1, source_target_pairs={{0,8},{2,10},{4,12},{6,14},{8,0},{10,2},{12,4},{14,6},{1,9},{3,11}... | collective-permute-start | bytes 4915208 | tf_op jit(solution)/shard_map/ppermute | solution.py:89
  349.1 72.6 %collective-permute-start.24 = (bf16[1280,640]{1,0:T(8,128)(2,1)S(1)}, bf16[1280,640]{1,0:T(8,128)(2,1)}, u32[]{:S(2)}, u32[]{:S(2)}) collective-permute-start(bf16[1280,640]{1,0:T(8,128)(2,1)S(1)} %select_dynamic-update-slice_fusion), channel_id=1, source_target_pairs={{0,1},{1,0},{2,3},{3,2},{4,5},{5,4},{6,7},{7,6},{8,9},{9,8},{10,11... | collective-permute-start | bytes 4915208 | tf_op jit(solution)/shard_map/ppermute | solution.py:92
  349.1 81.1 %collective-permute-start.27 = (bf16[1280,640]{1,0:T(8,128)(2,1)S(1)}, bf16[1280,640]{1,0:T(8,128)(2,1)}, u32[]{:S(2)}, u32[]{:S(2)}) collective-permute-start(bf16[1280,640]{1,0:T(8,128)(2,1)S(1)} %select_dynamic-update-slice_fusion), channel_id=1, source_target_pairs={{0,2},{2,0},{4,6},{6,4},{8,10},{10,8},{12,14},{14,12},{1,3},{3,1},... | collective-permute-start | bytes 4915208 | tf_op jit(solution)/shard_map/ppermute | solution.py:89
  420.3 37.0 %collective-permute-start.26 = (bf16[1280,640]{1,0:T(8,128)(2,1)}, bf16[1280,640]{1,0:T(8,128)(2,1)}, u32[]{:S(2)}, u32[]{:S(2)}) collective-permute-start(bf16[1280,640]{1,0:T(8,128)(2,1)} %collective-permute-done.25), channel_id=1, source_target_pairs={{0,2},{2,0},{4,6},{6,4},{8,10},{10,8},{12,14},{14,12},{1,3},{3,1},... | collective-permute-start | bytes 4915208 | tf_op jit(solution)/shard_map/ppermute | solution.py:89
  426.6 35.1 %collective-permute-start.32 = (bf16[640,640]{0,1:T(8,128)(2,1)S(1)}, bf16[640,640]{0,1:T(8,128)(2,1)S(1)}, u32[]{:S(2)}, u32[]{:S(2)}) collective-permute-start(bf16[640,640]{0,1:T(8,128)(2,1)S(1)} %convolution_convert_fusion), channel_id=1, source_target_pairs={{0,16},{16,0},{1,17},{17,1},{2,18},{18,2},{3,19},{19,3},{4,20},{20... | collective-permute-start | bytes 2457608 | tf_op jit(solution)/shard_map/ppermute | solution.py:92
  429.6 57.7 %collective-permute-start.31 = (bf16[640,640]{0,1:T(8,128)(2,1)S(1)}, bf16[640,640]{0,1:T(8,128)(2,1)S(1)}, u32[]{:S(2)}, u32[]{:S(2)}) collective-permute-start(bf16[640,640]{0,1:T(8,128)(2,1)S(1)} %convolution_convert_fusion.1), channel_id=1, source_target_pairs={{0,16},{16,0},{1,17},{17,1},{2,18},{18,2},{3,19},{19,3},{4,20},{20... | collective-permute-start | bytes 2457608 | tf_op jit(solution)/shard_map/ppermute | solution.py:92
  460.3 21.2 %collective-permute-start.29 = (bf16[640,640]{0,1:T(8,128)(2,1)S(1)}, bf16[640,640]{0,1:T(8,128)(2,1)S(1)}, u32[]{:S(2)}, u32[]{:S(2)}) collective-permute-start(bf16[640,640]{0,1:T(8,128)(2,1)S(1)} %convolution_convert_fusion.2), channel_id=1, source_target_pairs={{0,4},{2,6},{4,0},{6,2},{8,12},{10,14},{12,8},{14,10},{1,5},{3,7},... | collective-permute-start | bytes 2457608 | tf_op jit(solution)/shard_map/ppermute | solution.py:89
  463.4 35.7 %collective-permute-start.33 = (bf16[640,640]{0,1:T(8,128)(2,1)S(1)}, bf16[640,640]{0,1:T(8,128)(2,1)S(1)}, u32[]{:S(2)}, u32[]{:S(2)}) collective-permute-start(bf16[640,640]{0,1:T(8,128)(2,1)S(1)} %add_convert_fusion), channel_id=1, source_target_pairs={{0,4},{2,6},{4,0},{6,2},{8,12},{10,14},{12,8},{14,10},{1,5},{3,7},... | collective-permute-start | bytes 2457608 | tf_op jit(solution)/shard_map/ppermute | solution.py:89
  467.2 18.6 %copy-start.1 = (bf16[1280,640]{1,0:T(8,128)(2,1)S(1)}, bf16[1280,640]{1,0:T(8,128)(2,1)}, u32[]{:S(2)}) copy-start(bf16[1280,640]{1,0:T(8,128)(2,1)} %copy-done) | copy-start | bytes 4915204
  467.2 47.2 %collective-permute-start.28 = (bf16[640,640]{0,1:T(8,128)(2,1)S(1)}, bf16[640,640]{0,1:T(8,128)(2,1)S(1)}, u32[]{:S(2)}, u32[]{:S(2)}) collective-permute-start(bf16[640,640]{0,1:T(8,128)(2,1)S(1)} %convolution_convert_fusion.3), channel_id=1, source_target_pairs={{0,4},{2,6},{4,0},{6,2},{8,12},{10,14},{12,8},{14,10},{1,5},{3,7},... | collective-permute-start | bytes 2457608 | tf_op jit(solution)/shard_map/ppermute | solution.py:89
  484.5 29.9 %collective-permute-start.30 = (bf16[640,640]{0,1:T(8,128)(2,1)S(1)}, bf16[640,640]{0,1:T(8,128)(2,1)S(1)}, u32[]{:S(2)}, u32[]{:S(2)}) collective-permute-start(bf16[640,640]{0,1:T(8,128)(2,1)S(1)} %add_convert_fusion.1), channel_id=1, source_target_pairs={{0,16},{16,0},{1,17},{17,1},{2,18},{18,2},{3,19},{19,3},{4,20},{20... | collective-permute-start | bytes 2457608 | tf_op jit(solution)/shard_map/ppermute | solution.py:92
